TPU v7x, 32 devices: a whole 2x2x4 slice. The times are simulated.
32 devices in a mesh: groups: 2 (over y), prefill: 16 (over z, x, core).
Axes of the slice: x: 2, y: 2, z: 4, core: 2. Of those that a mesh axis runs over, the one named last changes fastest.
Arguments:
- queries: bfloat16 [4096, 8192], P(('groups', 'prefill')), parts along dimension 0, may hold values from -200 to 200, as said below
- keys: bfloat16 [4096, 8192], P(('groups', 'prefill')), parts along dimension 0, may hold values from -6 to 6
- values: bfloat16 [4096, 8192], P(('groups', 'prefill')), parts along dimension 0, may hold values from -24 to 24
- span_prompt: int32 [32], P('groups'), parts along dimension 0, may hold values from 0 to 4, never falling along the last dimension, each value on 1 to 6 neighbouring positions
- tails: int32 [10], P('groups'), parts along dimension 0, may hold values from 1 to 128, as said below
- owners: int32 [10], P('groups'), parts along dimension 0, may hold values from 0 to 15
Outputs:
- attended: bfloat16 [4096, 8192], P(('groups', 'prefill')), parts along dimension 0
- key_cache: bfloat16 [4096, 8192], P(('groups', 'prefill')), parts along dimension 0
- value_cache: bfloat16 [4096, 8192], P(('groups', 'prefill')), parts along dimension 0
There are 2 independent parts, one for each index of `groups`. A program takes and returns all parts, laid end to end along the dimension named above; each array names one. Nothing has to cross between parts.
Inputs may be any that keep to these rules, and one draw needn't show every extreme that they name: `queries`: queries are of order one; a few may be large. `tails`: the first prompt's last span is full. `span_prompt`: the spans of one prompt stand in a row, in order.
All inputs are finite; a program needn't handle non-finite values.
Results may differ from a plain program's by a relative error of at most 0.0032.
Values may be sent and summed in bfloat16 or wider, within the bound.
A program may use at most 128 MiB of HBM per device.

v0:
```python
import jax
import jax.numpy as jnp
from jax import lax
from jax.sharding import PartitionSpec as P

HEADS = 64
MAXC = 6


def from_behind(array, axis, by):
    devices = lax.axis_size(axis)
    pairs = [(i, i + by) for i in range(devices) if 0 <= i + by < devices]
    return lax.ppermute(array, axis, pairs)


def pick_entry(table, where_at):
    index = jnp.arange(table.shape[0], dtype=jnp.int32)
    return jnp.sum(jnp.where(index == where_at, table, 0))


def local(queries, keys, values, span_prompt, tails, owners):
    rows, width = queries.shape
    depth = width // HEADS
    count_dev = lax.axis_size("prefill")
    me_index = lax.axis_index("prefill")
    span_index = jnp.arange(span_prompt.shape[0], dtype=jnp.int32)
    prompt_id = pick_entry(span_prompt, me_index)
    mine = span_prompt == prompt_id
    order = jnp.sum(mine & (span_index < me_index))
    count = jnp.sum(mine)
    length = (count - 1) * rows + pick_entry(tails, prompt_id)
    owner = pick_entry(owners, prompt_id)
    local_rows = jnp.arange(rows, dtype=jnp.int32)
    query_pos = order * rows + local_rows
    used = query_pos < length
    blocks = [(keys, values)]
    carried = (keys, values)
    for step in range(1, MAXC):
        carried = from_behind((carried[0], carried[1]), "prefill", 1)
        blocks.append(carried)
    scale = 1.0 / depth**0.5
    query_heads = queries.reshape(rows, HEADS, depth)
    own_allowed = (local_rows[None, :] <= local_rows[:, None]) & (
        (order * rows + local_rows)[None, :] < length
    )
    scores = []
    allowed_list = []
    for step in range(MAXC):
        key_heads = blocks[step][0].reshape(rows, HEADS, depth)
        score = (
            jnp.einsum("qhd,khd->hqk", query_heads, key_heads, preferred_element_type=jnp.float32)
            * scale
        )
        if step == 0:
            allowed = own_allowed[None]
        else:
            allowed = jnp.broadcast_to(step <= order, (1, 1, 1))
        scores.append(score)
        allowed_list.append(allowed)
    top = jnp.full((HEADS, rows, 1), -jnp.inf, jnp.float32)
    for step in range(MAXC):
        masked = jnp.where(allowed_list[step], scores[step], -jnp.inf)
        top = jnp.maximum(top, jnp.max(masked, axis=-1, keepdims=True))
    total = jnp.zeros((HEADS, rows), jnp.float32)
    mixed = jnp.zeros((rows, HEADS, depth), jnp.float32)
    for step in range(MAXC):
        weight = jnp.where(allowed_list[step], jnp.exp(scores[step] - top), jnp.float32(0.0))
        total = total + jnp.sum(weight, axis=-1)
        value_heads = blocks[step][1].reshape(rows, HEADS, depth)
        mixed = mixed + jnp.einsum(
            "hqk,khd->qhd",
            weight.astype(jnp.bfloat16),
            value_heads,
            preferred_element_type=jnp.float32,
        )
    mixed = mixed / jnp.transpose(total)[:, :, None]
    mixed = jnp.where(used[:, None, None], mixed, jnp.float32(0.0))
    attended = mixed.reshape(rows, width).astype(jnp.bfloat16)
    masked_keys = jnp.where(used[:, None], keys, jnp.zeros_like(keys))
    masked_values = jnp.where(used[:, None], values, jnp.zeros_like(values))
    rolled_keys = jnp.roll(masked_keys.reshape(rows // count_dev, count_dev, width), owner, axis=1)
    rolled_values = jnp.roll(
        masked_values.reshape(rows // count_dev, count_dev, width), owner, axis=1
    )
    got_keys, got_values = (
        lax.all_to_all(rolled_keys, "prefill", split_axis=1, concat_axis=1, tiled=True),
        lax.all_to_all(rolled_values, "prefill", split_axis=1, concat_axis=1, tiled=True),
    )
    return (attended, got_keys.reshape(rows, width), got_values.reshape(rows, width))


def solution(mesh):
    placed = (
        P(("groups", "prefill"), None),
        P(("groups", "prefill"), None),
        P(("groups", "prefill"), None),
        P("groups"),
        P("groups"),
        P("groups"),
    )
    return jax.shard_map(
        local,
        mesh=mesh,
        in_specs=placed,
        out_specs=(
            P(("groups", "prefill"), None),
            P(("groups", "prefill"), None),
            P(("groups", "prefill"), None),
        ),
        check_vma=False,
    )
```

profile of v0, /device:TPU:15, one launch (start us, length us, event | category | flops | bytes accessed | tf_op | source)
XLA Modules:
  0.0 363.1 jit_solution(2950724669691196012)
XLA Ops:
  0.7 4.2 %copy.83 = bf16[128,8192]{0,1:T(8,128)(2,1)} copy(bf16[128,8192]{1,0:T(8,128)(2,1)} %param.9) | data formatting | bytes 4194304 | tf_op args[1]
  13.9 4.6 %broadcast_select_fusion = (bf16[128,8192]{1,0:T(8,128)(2,1)}, bf16[128,8192]{1,0:T(8,128)(2,1)}) fusion(bf16[128,8192]{1,0:T(8,128)(2,1)} %param.10, pred[128]{0:T(512)(128)(4,1)S(1)} %add_compare_fusion, bf16[128,8192]{1,0:T(8,128)(2,1)} %param.9), kind=kLoop, calls=%fused_computation.70 | loop fusion | flops 2097152 | bytes 8388736 | tf_op jit(solution)/shard_map/jit(_where)/select_n | solution.py:80
  26.1 5.0 %all-to-all-start = ((bf16[8,16,8192]{2,0,1:T(8,128)(2,1)}), bf16[8,16,8192]{2,0,1:T(8,128)(2,1)}, u32[]{:S(2)}, u32[]{:S(2)}) async-start(bf16[8,16,8192]{2,0,1:T(8,128)(2,1)} %copy.106), calls=%async_computation | async-start | bytes 4194304 | tf_op jit(solution)/shard_map/all_to_all | solution.py:86
  37.2 62.3 %collective-permute-done.5 = bf16[128,8192]{1,0:T(8,128)(2,1)} collective-permute-done((bf16[128,8192]{1,0:T(8,128)(2,1)}, bf16[128,8192]{1,0:T(8,128)(2,1)}, u32[]{:S(2)}, u32[]{:S(2)}) %collective-permute-start.5) | collective-permute-done | bytes 2097184 | tf_op jit(solution)/shard_map/ppermute | solution.py:13
  99.4 5.3 %collective-permute-start.6 = (bf16[128,8192]{1,0:T(8,128)(2,1)}, bf16[128,8192]{1,0:T(8,128)(2,1)}, u32[]{:S(2)}, u32[]{:S(2)}) collective-permute-start(bf16[128,8192]{1,0:T(8,128)(2,1)} %collective-permute-done.5), channel_id=1, source_target_pairs={{0,1},{1,2},{2,3},{3,4},{4,5},{5,6},{6,7},{7,8},{8,9},{9,10},{10,1... | collective-permute-start | bytes 6291464 | tf_op jit(solution)/shard_map/ppermute | solution.py:13
  104.7 17.2 %collective-permute-done.1 = bf16[128,8192]{0,1:T(8,128)(2,1)} collective-permute-done((bf16[128,8192]{0,1:T(8,128)(2,1)}, bf16[128,8192]{0,1:T(8,128)(2,1)}, u32[]{:S(2)}, u32[]{:S(2)}) %collective-permute-start.1) | collective-permute-done | bytes 2097184 | tf_op jit(solution)/shard_map/ppermute | solution.py:13
  121.9 5.3 %collective-permute-start.2 = (bf16[128,8192]{0,1:T(8,128)(2,1)}, bf16[128,8192]{0,1:T(8,128)(2,1)}, u32[]{:S(2)}, u32[]{:S(2)}) collective-permute-start(bf16[128,8192]{0,1:T(8,128)(2,1)} %collective-permute-done.1), channel_id=1, source_target_pairs={{0,1},{1,2},{2,3},{3,4},{4,5},{5,6},{6,7},{7,8},{8,9},{9,10},{10,1... | collective-permute-start | bytes 6291464 | tf_op jit(solution)/shard_map/ppermute | solution.py:13
  133.0 4.3 %all-to-all-start.1 = ((bf16[8,16,8192]{2,0,1:T(8,128)(2,1)}), bf16[8,16,8192]{2,0,1:T(8,128)(2,1)}, u32[]{:S(2)}, u32[]{:S(2)}) async-start(bf16[8,16,8192]{2,0,1:T(8,128)(2,1)} %copy.108), calls=%async_computation.1 | async-start | bytes 4194304 | tf_op jit(solution)/shard_map/all_to_all | solution.py:87
  137.3 18.7 %collective-permute-done.6 = bf16[128,8192]{1,0:T(8,128)(2,1)} collective-permute-done((bf16[128,8192]{1,0:T(8,128)(2,1)}, bf16[128,8192]{1,0:T(8,128)(2,1)}, u32[]{:S(2)}, u32[]{:S(2)}) %collective-permute-start.6) | collective-permute-done | bytes 2097184 | tf_op jit(solution)/shard_map/ppermute | solution.py:13
  156.0 5.3 %collective-permute-start.7 = (bf16[128,8192]{1,0:T(8,128)(2,1)}, bf16[128,8192]{1,0:T(8,128)(2,1)}, u32[]{:S(2)}, u32[]{:S(2)}) collective-permute-start(bf16[128,8192]{1,0:T(8,128)(2,1)} %collective-permute-done.6), channel_id=1, source_target_pairs={{0,1},{1,2},{2,3},{3,4},{4,5},{5,6},{6,7},{7,8},{8,9},{9,10},{10,1... | collective-permute-start | bytes 6291464 | tf_op jit(solution)/shard_map/ppermute | solution.py:13
  161.3 39.3 %collective-permute-done.2 = bf16[128,8192]{0,1:T(8,128)(2,1)} collective-permute-done((bf16[128,8192]{0,1:T(8,128)(2,1)}, bf16[128,8192]{0,1:T(8,128)(2,1)}, u32[]{:S(2)}, u32[]{:S(2)}) %collective-permute-start.2) | collective-permute-done | bytes 2097184 | tf_op jit(solution)/shard_map/ppermute | solution.py:13
  200.6 5.3 %collective-permute-start.3 = (bf16[128,8192]{0,1:T(8,128)(2,1)}, bf16[128,8192]{0,1:T(8,128)(2,1)}, u32[]{:S(2)}, u32[]{:S(2)}) collective-permute-start(bf16[128,8192]{0,1:T(8,128)(2,1)} %collective-permute-done.2), channel_id=1, source_target_pairs={{0,1},{1,2},{2,3},{3,4},{4,5},{5,6},{6,7},{7,8},{8,9},{9,10},{10,1... | collective-permute-start | bytes 6291464 | tf_op jit(solution)/shard_map/ppermute | solution.py:13
  205.8 28.5 %collective-permute-done.7 = bf16[128,8192]{1,0:T(8,128)(2,1)} collective-permute-done((bf16[128,8192]{1,0:T(8,128)(2,1)}, bf16[128,8192]{1,0:T(8,128)(2,1)}, u32[]{:S(2)}, u32[]{:S(2)}) %collective-permute-start.7) | collective-permute-done | bytes 2097184 | tf_op jit(solution)/shard_map/ppermute | solution.py:13
  234.4 5.3 %collective-permute-start.8 = (bf16[128,8192]{1,0:T(8,128)(2,1)}, bf16[128,8192]{1,0:T(8,128)(2,1)}, u32[]{:S(2)}, u32[]{:S(2)}) collective-permute-start(bf16[128,8192]{1,0:T(8,128)(2,1)} %collective-permute-done.7), channel_id=1, source_target_pairs={{0,1},{1,2},{2,3},{3,4},{4,5},{5,6},{6,7},{7,8},{8,9},{9,10},{10,1... | collective-permute-start | bytes 6291464 | tf_op jit(solution)/shard_map/ppermute | solution.py:13
  239.6 4.1 %copy.122 = bf16[128,8192]{0,1:T(8,128)(2,1)} copy(bf16[128,8192]{1,0:T(8,128)(2,1)} %param.10) | data formatting | bytes 4194304 | tf_op jit(solution)/shard_map/reshape | solution.py:69
  247.0 9.8 %collective-permute-done.3 = bf16[128,8192]{0,1:T(8,128)(2,1)} collective-permute-done((bf16[128,8192]{0,1:T(8,128)(2,1)}, bf16[128,8192]{0,1:T(8,128)(2,1)}, u32[]{:S(2)}, u32[]{:S(2)}) %collective-permute-start.3) | collective-permute-done | bytes 2097184 | tf_op jit(solution)/shard_map/ppermute | solution.py:13
  256.8 5.5 %collective-permute-start.4 = (bf16[128,8192]{0,1:T(8,128)(2,1)}, bf16[128,8192]{0,1:T(8,128)(2,1)}, u32[]{:S(2)}, u32[]{:S(2)}) collective-permute-start(bf16[128,8192]{0,1:T(8,128)(2,1)} %collective-permute-done.3), channel_id=1, source_target_pairs={{0,1},{1,2},{2,3},{3,4},{4,5},{5,6},{6,7},{7,8},{8,9},{9,10},{10,1... | collective-permute-start | bytes 6291464 | tf_op jit(solution)/shard_map/ppermute | solution.py:13
  262.3 5.2 %select_reduce_fusion.5 = (f32[64,128]{1,0:T(8,128)S(1)}, f32[64,128,128]{1,2,0:T(8,128)}) fusion(pred[128,128]{0,1:T(8,128)(4,1)S(1)} %fusion.71, bf16[128,8192]{1,0:T(8,128)(2,1)} %param.9, bf16[128,8192]{1,0:T(8,128)(2,1)S(1)} %copy-done), kind=kOutput, calls=%fused_computation.18 | convolution fusion | flops 271572992 | bytes 8437760 | tf_op jit(solution)/shard_map/qhd,khd->hqk/dot_general | solution.py:51
  267.5 4.1 %copy.96 = bf16[128,8192]{0,1:T(8,128)(2,1)} copy(bf16[128,8192]{1,0:T(8,128)(2,1)} %collective-permute-done.5) | data formatting | bytes 4194304 | tf_op jit(solution)/shard_map/ppermute | solution.py:13
  271.6 5.2 %select_reduce_fusion.4 = (f32[64,128]{1,0:T(8,128)S(1)}, f32[64,128,128]{1,2,0:T(8,128)}) fusion(pred[]{:T(512)S(6)} %ge.15, bf16[128,64,128]{0,2,1:T(8,128)(2,1)} %bitcast, bf16[128,8192]{1,0:T(8,128)(2,1)S(1)} %copy-done), kind=kOutput, calls=%fused_computation.17 | convolution fusion | flops 271572992 | bytes 8421377 | tf_op jit(solution)/shard_map/qhd,khd->hqk/dot_general | solution.py:51
  276.7 4.1 %copy.107 = bf16[8,16,8192]{2,1,0:T(8,128)(2,1)} copy(bf16[8,16,8192]{2,0,1:T(8,128)(2,1)} %all-to-all-done) | data formatting | bytes 4194304 | tf_op jit(solution)/shard_map/all_to_all | solution.py:86
  280.8 4.1 %copy.109 = bf16[8,16,8192]{2,1,0:T(8,128)(2,1)} copy(bf16[8,16,8192]{2,0,1:T(8,128)(2,1)} %all-to-all-done.1) | data formatting | bytes 4194304 | tf_op jit(solution)/shard_map/all_to_all | solution.py:87
  284.9 4.1 %copy.98 = bf16[128,8192]{0,1:T(8,128)(2,1)} copy(bf16[128,8192]{1,0:T(8,128)(2,1)} %collective-permute-done.6) | data formatting | bytes 4194304 | tf_op jit(solution)/shard_map/ppermute | solution.py:13
  289.0 5.1 %select_reduce_fusion.3 = (f32[64,128]{1,0:T(8,128)S(1)}, f32[64,128,128]{1,2,0:T(8,128)}) fusion(pred[]{:T(512)S(6)} %ge.16, bf16[128,64,128]{0,2,1:T(8,128)(2,1)} %bitcast.1, bf16[128,8192]{1,0:T(8,128)(2,1)S(1)} %copy-done), kind=kOutput, calls=%fused_computation.16 | convolution fusion | flops 271572992 | bytes 8421377 | tf_op jit(solution)/shard_map/qhd,khd->hqk/dot_general | solution.py:51
  294.1 4.1 %copy.100 = bf16[128,8192]{0,1:T(8,128)(2,1)} copy(bf16[128,8192]{1,0:T(8,128)(2,1)} %collective-permute-done.7) | data formatting | bytes 4194304 | tf_op jit(solution)/shard_map/ppermute | solution.py:13
  298.2 5.2 %select_reduce_fusion.2 = (f32[64,128]{1,0:T(8,128)S(1)}, f32[64,128,128]{1,2,0:T(8,128)}) fusion(pred[]{:T(512)S(6)} %ge.17, bf16[128,64,128]{0,2,1:T(8,128)(2,1)} %bitcast.2, bf16[128,8192]{1,0:T(8,128)(2,1)S(1)} %copy-done), kind=kOutput, calls=%fused_computation.15 | convolution fusion | flops 271572992 | bytes 8421377 | tf_op jit(solution)/shard_map/qhd,khd->hqk/dot_general | solution.py:51
  303.4 4.1 %copy.102 = bf16[128,8192]{0,1:T(8,128)(2,1)} copy(bf16[128,8192]{1,0:T(8,128)(2,1)} %collective-permute-done.8) | data formatting | bytes 4194304 | tf_op jit(solution)/shard_map/ppermute | solution.py:13
  322.9 6.4 %fusion.4 = (f32[64,128]{1,0:T(8,128)S(1)}, f32[64,128]{1,0:T(8,128)S(1)}, f32[64,128]{1,0:T(8,128)S(1)}, f32[64,128]{1,0:T(8,128)S(1)}, f32[64,128]{1,0:T(8,128)S(1)}, /*index=5*/f32[64,128]{1,0:T(8,128)S(1)}) fusion(f32[64,128,128]{1,2,0:T(8,128)S(1)} %copy-done.2, f32[64,128]{1,0:T(8,128)S(1)} %maximum_maximum_fusion, pred[]{:T(512)S(6)} %ge.15, ...), kind=kLoop, calls=%fused_computation.21 | loop fusion | flops 25116672 | bytes 25411588 | tf_op jit(solution)/shard_map/reduce_sum | solution.py:68
  329.3 4.7 %fusion.17 = f32[64,128,128]{1,2,0:T(8,128)} fusion(bf16[128,64,128]{0,2,1:T(8,128)(2,1)} %bitcast.94, f32[64,128,128]{1,2,0:T(8,128)S(1)} %copy-done.4, f32[64,128]{1,0:T(8,128)S(1)} %maximum_maximum_fusion, pred[]{:T(512)S(6)} %ge.17), kind=kOutput, calls=%fused_computation.32 | convolution fusion | flops 272629760 | bytes 10518529 | tf_op jit(solution)/shard_map/hqk,khd->qhd/dot_general | solution.py:70
  342.6 4.1 %copy.104 = bf16[128,8192]{0,1:T(8,128)(2,1)} copy(bf16[128,8192]{1,0:T(8,128)(2,1)} %collective-permute-done.9) | data formatting | bytes 4194304 | tf_op jit(solution)/shard_map/ppermute | solution.py:13
  346.6 12.4 %fusion.1 = bf16[128,64,128]{0,2,1:T(8,128)(2,1)} fusion(f32[64,128,128]{1,2,0:T(8,128)} %fusion.15, f32[64,128,128]{1,2,0:T(8,128)} %fusion.17, f32[64,128,128]{1,2,0:T(8,128)} %fusion.19, f32[64,128,128]{1,2,0:T(8,128)} %fusion.23, f32[64,128,128]{1,2,0:T(8,128)} %fusion.21, bf16[128,64,128]{0,2,1:T(8,128)(2,1)} %bitcast.89, ...), kind=kOutput, calls=%fused_computation.6 | convolution fusion | flops 281018368 | bytes 29425792 | tf_op jit(solution)/shard_map/hqk,khd->qhd/dot_general | solution.py:70
  359.1 4.1 %copy.110 = bf16[128,8192]{1,0:T(8,128)(2,1)} copy(bf16[128,8192]{0,1:T(8,128)(2,1)} %bitcast.90) | data formatting | bytes 4194304
  (55 shorter events, 48.7 us)
Async XLA Ops:
  0.6 261.7 %copy-start = (bf16[128,8192]{1,0:T(8,128)(2,1)S(1)}, bf16[128,8192]{1,0:T(8,128)(2,1)}, u32[]{:S(2)}) copy-start(bf16[128,8192]{1,0:T(8,128)(2,1)} %param.8) | copy-start | bytes 6291460
  0.6 8.0 %copy-start.11 = (s32[16]{0:T(128)S(1)}, s32[16]{0:T(128)}, u32[]{:S(2)}) copy-start(s32[16]{0:T(128)} %param.11) | copy-start | bytes 196
  0.7 11.2 %copy-start.12 = (s32[5]{0:T(128)S(1)}, s32[5]{0:T(128)}, u32[]{:S(2)}) copy-start(s32[5]{0:T(128)} %param.12) | copy-start | bytes 64
  0.7 11.2 %copy-start.13 = (s32[5]{0:T(128)S(1)}, s32[5]{0:T(128)}, u32[]{:S(2)}) copy-start(s32[5]{0:T(128)} %param.13) | copy-start | bytes 64
  4.9 29.5 %collective-permute-start = (bf16[128,8192]{0,1:T(8,128)(2,1)}, bf16[128,8192]{0,1:T(8,128)(2,1)}, u32[]{:S(2)}, u32[]{:S(2)}) collective-permute-start(bf16[128,8192]{0,1:T(8,128)(2,1)} %copy.83), channel_id=1, source_target_pairs={{0,1},{1,2},{2,3},{3,4},{4,5},{5,6},{6,7},{7,8},{8,9},{9,10},{10,1... | collective-permute-start | bytes 6291464 | tf_op jit(solution)/shard_map/ppermute | solution.py:13
  26.1 106.9 %all-to-all-start = ((bf16[8,16,8192]{2,0,1:T(8,128)(2,1)}), bf16[8,16,8192]{2,0,1:T(8,128)(2,1)}, u32[]{:S(2)}, u32[]{:S(2)}) async-start(bf16[8,16,8192]{2,0,1:T(8,128)(2,1)} %copy.106), calls=%async_computation | async-start | bytes 4194304 | tf_op jit(solution)/shard_map/all_to_all | solution.py:86
  31.1 68.4 %collective-permute-start.5 = (bf16[128,8192]{1,0:T(8,128)(2,1)}, bf16[128,8192]{1,0:T(8,128)(2,1)}, u32[]{:S(2)}, u32[]{:S(2)}) collective-permute-start(bf16[128,8192]{1,0:T(8,128)(2,1)} %param.10), channel_id=1, source_target_pairs={{0,1},{1,2},{2,3},{3,4},{4,5},{5,6},{6,7},{7,8},{8,9},{9,10},{10,1... | collective-permute-start | bytes 6291464 | tf_op jit(solution)/shard_map/ppermute | solution.py:13
  34.4 87.5 %collective-permute-start.1 = (bf16[128,8192]{0,1:T(8,128)(2,1)}, bf16[128,8192]{0,1:T(8,128)(2,1)}, u32[]{:S(2)}, u32[]{:S(2)}) collective-permute-start(bf16[128,8192]{0,1:T(8,128)(2,1)} %collective-permute-done), channel_id=1, source_target_pairs={{0,1},{1,2},{2,3},{3,4},{4,5},{5,6},{6,7},{7,8},{8,9},{9,10},{10,1... | collective-permute-start | bytes 6291464 | tf_op jit(solution)/shard_map/ppermute | solution.py:13
  99.4 56.6 %collective-permute-start.6 = (bf16[128,8192]{1,0:T(8,128)(2,1)}, bf16[128,8192]{1,0:T(8,128)(2,1)}, u32[]{:S(2)}, u32[]{:S(2)}) collective-permute-start(bf16[128,8192]{1,0:T(8,128)(2,1)} %collective-permute-done.5), channel_id=1, source_target_pairs={{0,1},{1,2},{2,3},{3,4},{4,5},{5,6},{6,7},{7,8},{8,9},{9,10},{10,1... | collective-permute-start | bytes 6291464 | tf_op jit(solution)/shard_map/ppermute | solution.py:13
  121.9 78.6 %collective-permute-start.2 = (bf16[128,8192]{0,1:T(8,128)(2,1)}, bf16[128,8192]{0,1:T(8,128)(2,1)}, u32[]{:S(2)}, u32[]{:S(2)}) collective-permute-start(bf16[128,8192]{0,1:T(8,128)(2,1)} %collective-permute-done.1), channel_id=1, source_target_pairs={{0,1},{1,2},{2,3},{3,4},{4,5},{5,6},{6,7},{7,8},{8,9},{9,10},{10,1... | collective-permute-start | bytes 6291464 | tf_op jit(solution)/shard_map/ppermute | solution.py:13
  133.0 147.8 %all-to-all-start.1 = ((bf16[8,16,8192]{2,0,1:T(8,128)(2,1)}), bf16[8,16,8192]{2,0,1:T(8,128)(2,1)}, u32[]{:S(2)}, u32[]{:S(2)}) async-start(bf16[8,16,8192]{2,0,1:T(8,128)(2,1)} %copy.108), calls=%async_computation.1 | async-start | bytes 4194304 | tf_op jit(solution)/shard_map/all_to_all | solution.py:87
  156.0 78.4 %collective-permute-start.7 = (bf16[128,8192]{1,0:T(8,128)(2,1)}, bf16[128,8192]{1,0:T(8,128)(2,1)}, u32[]{:S(2)}, u32[]{:S(2)}) collective-permute-start(bf16[128,8192]{1,0:T(8,128)(2,1)} %collective-permute-done.6), channel_id=1, source_target_pairs={{0,1},{1,2},{2,3},{3,4},{4,5},{5,6},{6,7},{7,8},{8,9},{9,10},{10,1... | collective-permute-start | bytes 6291464 | tf_op jit(solution)/shard_map/ppermute | solution.py:13
  200.6 56.3 %collective-permute-start.3 = (bf16[128,8192]{0,1:T(8,128)(2,1)}, bf16[128,8192]{0,1:T(8,128)(2,1)}, u32[]{:S(2)}, u32[]{:S(2)}) collective-permute-start(bf16[128,8192]{0,1:T(8,128)(2,1)} %collective-permute-done.2), channel_id=1, source_target_pairs={{0,1},{1,2},{2,3},{3,4},{4,5},{5,6},{6,7},{7,8},{8,9},{9,10},{10,1... | collective-permute-start | bytes 6291464 | tf_op jit(solution)/shard_map/ppermute | solution.py:13
  234.4 69.1 %collective-permute-start.8 = (bf16[128,8192]{1,0:T(8,128)(2,1)}, bf16[128,8192]{1,0:T(8,128)(2,1)}, u32[]{:S(2)}, u32[]{:S(2)}) collective-permute-start(bf16[128,8192]{1,0:T(8,128)(2,1)} %collective-permute-done.7), channel_id=1, source_target_pairs={{0,1},{1,2},{2,3},{3,4},{4,5},{5,6},{6,7},{7,8},{8,9},{9,10},{10,1... | collective-permute-start | bytes 6291464 | tf_op jit(solution)/shard_map/ppermute | solution.py:13
  256.8 56.2 %collective-permute-start.4 = (bf16[128,8192]{0,1:T(8,128)(2,1)}, bf16[128,8192]{0,1:T(8,128)(2,1)}, u32[]{:S(2)}, u32[]{:S(2)}) collective-permute-start(bf16[128,8192]{0,1:T(8,128)(2,1)} %collective-permute-done.3), channel_id=1, source_target_pairs={{0,1},{1,2},{2,3},{3,4},{4,5},{5,6},{6,7},{7,8},{8,9},{9,10},{10,1... | collective-permute-start | bytes 6291464 | tf_op jit(solution)/shard_map/ppermute | solution.py:13
  307.5 35.1 %collective-permute-start.9 = (bf16[128,8192]{1,0:T(8,128)(2,1)}, bf16[128,8192]{1,0:T(8,128)(2,1)}, u32[]{:S(2)}, u32[]{:S(2)}) collective-permute-start(bf16[128,8192]{1,0:T(8,128)(2,1)} %collective-permute-done.8), channel_id=1, source_target_pairs={{0,1},{1,2},{2,3},{3,4},{4,5},{5,6},{6,7},{7,8},{8,9},{9,10},{10,1... | collective-permute-start | bytes 6291464 | tf_op jit(solution)/shard_map/ppermute | solution.py:13
  309.6 6.8 %copy-start.10 = (bf16[128,8192]{0,1:T(8,128)(2,1)S(1)}, bf16[128,8192]{0,1:T(8,128)(2,1)}, u32[]{:S(2)}) copy-start(bf16[128,8192]{0,1:T(8,128)(2,1)} %copy.102) | copy-start | bytes 6291460
  313.0 7.5 %copy-start.4 = (f32[64,128,128]{1,2,0:T(8,128)S(1)}, f32[64,128,128]{1,2,0:T(8,128)}, u32[]{:S(2)}) copy-start(f32[64,128,128]{1,2,0:T(8,128)} %get-tuple-element.31) | copy-start | bytes 12582916
  313.0 7.5 %copy-start.6 = (f32[64,128,128]{1,2,0:T(8,128)S(1)}, f32[64,128,128]{1,2,0:T(8,128)}, u32[]{:S(2)}) copy-start(f32[64,128,128]{1,2,0:T(8,128)} %get-tuple-element.35) | copy-start | bytes 12582916
  316.4 4.1 %copy-start.5 = (f32[64,128,128]{1,2,0:T(8,128)}, f32[64,128,128]{1,2,0:T(8,128)S(1)}, u32[]{:S(2)}) copy-start(f32[64,128,128]{1,2,0:T(8,128)S(1)} %get-tuple-element.27) | copy-start | bytes 12582916
  316.4 5.2 %copy-start.2 = (f32[64,128,128]{1,2,0:T(8,128)S(1)}, f32[64,128,128]{1,2,0:T(8,128)}, u32[]{:S(2)}) copy-start(f32[64,128,128]{1,2,0:T(8,128)} %get-tuple-element.37) | copy-start | bytes 12582916
  316.4 6.4 %copy-start.3 = (f32[64,128,128]{1,2,0:T(8,128)S(1)}, f32[64,128,128]{1,2,0:T(8,128)}, u32[]{:S(2)}) copy-start(f32[64,128,128]{1,2,0:T(8,128)} %get-tuple-element.33) | copy-start | bytes 12582916
  329.3 4.7 %copy-start.9 = (bf16[128,8192]{0,1:T(8,128)(2,1)S(1)}, bf16[128,8192]{0,1:T(8,128)(2,1)}, u32[]{:S(2)}) copy-start(bf16[128,8192]{0,1:T(8,128)(2,1)} %copy.98) | copy-start | bytes 6291460
  334.0 2.8 copy-start.8
  336.8 2.8 copy-start.7
  346.6 16.5 %copy-start.1 = (bf16[128,8192]{1,0:T(8,128)(2,1)S(1)}, bf16[128,8192]{1,0:T(8,128)(2,1)}, u32[]{:S(2)}) copy-start(bf16[128,8192]{1,0:T(8,128)(2,1)} %param.8) | copy-start | bytes 6291460
where the time goes:
time: 364 us; the launch traced here: 363 us
  waiting for transfers between devices  176 us (48%)
  matrix products  56.1 us (15%)
  starting transfers between devices  53.1 us (15%)
  local copies, waits for them, and re-layouts  49.3 us (14%)
  other arithmetic  20.9 us (6%)
  between operations  7.92 us (2%)
    ppermute x10, waiting for transfers between devices, from_behind(): return lax.ppermute(array, axis, pairs)  176 us
    ppermute x10, starting transfers between devices, from_behind(): return lax.ppermute(array, axis, pairs)  43.8 us
    dot_general x6, matrix products, local(): jnp.einsum('hqk,khd->qhd', weight.astype(jnp.bfloat16), value_heads, pref...  28.7 us
    dot_general x6, matrix products, local(): jnp.einsum('qhd,khd->hqk', query_heads, key_heads, preferred_element_type...  27.4 us
    ppermute x5, local copies, waits for them, and re-layouts, from_behind(): return lax.ppermute(array, axis, pairs)  20.4 us
    unnamed x30, local copies, waits for them, and re-layouts  11.8 us
  transfers between devices with their start and end apart: 12, of which 6 were waited for; matrix products, arithmetic and copies ran while one was open for 27% of the time, Pallas kernels for 0%

commit v1 on v0

--- a/solution.py
+++ b/solution.py
@@ -1,10 +1,16 @@
+import functools
 import jax
 import jax.numpy as jnp
 from jax import lax
+from jax.experimental import pallas as pl
+from jax.experimental.pallas import tpu as pltpu
 from jax.sharding import PartitionSpec as P
 
 HEADS = 64
 MAXC = 6
+CHUNKS = 4
+SLOTS = 5
+MESH = pl.DeviceIdType.MESH
 
 
 def from_behind(array, axis, by):
@@ -89,6 +95,302 @@
     return (attended, got_keys.reshape(rows, width), got_values.reshape(rows, width))
 
 
+def exchange_kernel(
+    sp, tails, owners, q_ref, k_ref, v_ref, att_ref, got_ref,
+    packed, slots, recv, send_a, send_b, recv_r, send_r, send_f, send_x, local_sem,
+):
+    rows, width = q_ref.shape
+    depth = width // HEADS
+    cw = width // CHUNKS
+    me = lax.axis_index("prefill")
+    z, x, c = me // 4, (me // 2) % 2, me % 2
+    sibling = me + 1 - 2 * c
+    others = [lax.rem(me + k, 16) for k in range(1, 16)]
+
+    prompt = sp[me]
+    order = jnp.int32(0)
+    count = jnp.int32(0)
+    for j in range(16):
+        same = jnp.where(sp[j] == prompt, 1, 0)
+        count = count + same
+        order = order + jnp.where(j < me, same, 0)
+    used_rows = (count - 1 - order) * rows + tails[prompt]
+    owner = owners[prompt]
+    spans = [
+        4 * z - 4 * (1 - x),
+        4 * z - 4 * (1 - x) + 1,
+        4 * z - 2,
+        4 * z - 1,
+        jnp.where(c == 1, me - 1, me - 5),
+    ]
+    flags = [
+        jnp.where(s >= 0, jnp.where(sp[jnp.maximum(s, 0)] == prompt, 1, 0), 0) for s in spans
+    ]
+
+    def clear(slot):
+        @pl.loop(0, 2 * width // 512)
+        def _(n):
+            slots[slot, :, pl.ds(pl.multiple_of(n * 512, 512), 512)] = jnp.zeros(
+                (rows, 512), jnp.bfloat16
+            )
+
+    for s in range(SLOTS):
+        pl.when(spans[s] < 0)(functools.partial(clear, s))
+
+    barrier = pltpu.get_barrier_semaphore()
+    for other in others:
+        pl.semaphore_signal(barrier, inc=1, device_id={"prefill": other}, device_id_type=MESH)
+    pl.semaphore_wait(barrier, 15)
+
+    def remote(src, dst, ssem, rsem, to):
+        return pltpu.make_async_remote_copy(
+            src_ref=src, dst_ref=dst, send_sem=ssem, recv_sem=rsem,
+            device_id={"prefill": to}, device_id_type=MESH,
+        )
+
+    started = []
+
+    def go(cond, copy):
+        pl.when(cond)(copy.start)
+        started.append((cond, copy))
+
+    def cols(ch):
+        return pl.ds(ch * 2 * cw, 2 * cw)
+
+    zslot = 2 * x + c
+
+    r = lax.broadcasted_iota(jnp.int32, (rows, rows), 0)
+    t = lax.broadcasted_iota(jnp.int32, (rows, rows), 1)
+    wanted = (((r >> 3) - owner) & 15) + ((r & 7) << 4)
+    moves = jnp.where((t == wanted) & (t < used_rows), 1.0, 0.0).astype(jnp.bfloat16)
+    for ch in range(CHUNKS):
+        for part, ref in ((0, k_ref), (1, v_ref)):
+            @pl.loop(0, cw // 256)
+            def _(n, ch=ch, part=part, ref=ref):
+                at = pl.multiple_of(n * 256, 256)
+                block = ref[:, pl.ds(ch * cw + at, 256)]
+                packed[:, pl.ds((2 * ch + part) * cw + at, 256)] = jnp.dot(
+                    moves, block, preferred_element_type=jnp.float32
+                ).astype(jnp.bfloat16)
+
+        own = packed.at[:, cols(ch)]
+        go(z < 3, remote(own, slots.at[zslot, :, cols(ch)], send_a.at[0, ch],
+                         recv.at[zslot, ch], lax.rem(me + 4, 16)))
+        go(x == 0, remote(own, slots.at[c, :, cols(ch)], send_a.at[1, ch],
+                          recv.at[c, ch], lax.rem(me + 2, 16)))
+        go(c == 0, remote(own, slots.at[4, :, cols(ch)], send_a.at[2, ch],
+                          recv.at[4, ch], sibling))
+
+    def block(ref, chip):
+        return ref.at[pl.ds(pl.multiple_of(chip * 16, 16), 16), :]
+
+    my_chip = me // 2
+    keep = pltpu.make_async_copy(block(packed, my_chip), got_ref.at[me], local_sem.at[4])
+    keep.start()
+    go(me >= 0, remote(block(packed, my_chip), got_ref.at[me], send_r.at[7], recv_r.at[me], sibling))
+    go(x == 1, remote(block(packed, lax.rem(my_chip + 7, 8)), got_ref.at[me], send_r.at[6],
+                      recv_r.at[me], lax.rem(me + 14, 16)))
+    for zp in (2, 1, 0):
+        for xp in range(2):
+            go(zp < z, remote(block(packed, 2 * zp + xp), got_ref.at[me], send_r.at[2 * zp + xp],
+                              recv_r.at[me], lax.rem(4 * zp + 2 * xp + c, 16)))
+
+    def arrived(slot, ch):
+        ref = slots.at[slot, :, cols(ch)]
+        pltpu.make_async_copy(ref, ref, recv.at[slot, ch]).wait()
+
+    def relay(ch):
+        @pl.when(z >= 1)
+        def _():
+            arrived(zslot, ch)
+        here = slots.at[zslot, :, cols(ch)]
+        go((z >= 1) & (x == 1), remote(here, slots.at[2 + c, :, cols(ch)], send_b.at[0, ch],
+                                       recv.at[2 + c, ch], lax.rem(me + 14, 16)))
+        go((z >= 1) & (x == 0) & (c == 1), remote(here, slots.at[4, :, cols(ch)], send_b.at[1, ch],
+                                                  recv.at[4, ch], lax.rem(me + 1, 16)))
+        go(z >= 1, remote(here, slots.at[zslot, :, cols(ch)], send_b.at[2, ch],
+                          recv.at[zslot, ch], sibling))
+        second = 2 * (1 - x) + c
+        has = (x == 1) | (z >= 1)
+
+        @pl.when(has)
+        def _():
+            arrived(second, ch)
+        there = slots.at[second, :, cols(ch)]
+        go((x == 0) & (z >= 1) & (z < 3) & (c == 1),
+           remote(there, slots.at[4, :, cols(ch)], send_b.at[3, ch], recv.at[4, ch],
+                  lax.rem(me + 3, 16)))
+        go(has, remote(there, slots.at[second, :, cols(ch)], send_b.at[4, ch],
+                       recv.at[second, ch], sibling))
+
+    scale = 1.0 / depth**0.5
+    causal = (t <= r) & (t < used_rows)
+    keep_row = lax.broadcasted_iota(jnp.int32, (rows, depth), 0) < used_rows
+    masks = [jnp.full((rows, rows), f, jnp.int32) > 0 for f in flags]
+
+    def attention(ch):
+        @pl.when(z >= 1)
+        def _():
+            arrived(2 * x + (1 - c), ch)
+
+        @pl.when((x == 1) | (z >= 1))
+        def _():
+            arrived(2 * (1 - x) + (1 - c), ch)
+
+        @pl.when(spans[4] >= 0)
+        def _():
+            arrived(4, ch)
+
+        @pl.loop(0, HEADS // CHUNKS)
+        def _(n):
+            at = pl.multiple_of(n * depth, depth)
+            mine = pl.ds(ch * cw + at, depth)
+            kcols = pl.ds(2 * ch * cw + at, depth)
+            vcols = pl.ds((2 * ch + 1) * cw + at, depth)
+            q = q_ref[:, mine]
+            dims = (((1,), (1,)), ((), ()))
+            scores = [
+                jnp.where(causal, lax.dot_general(
+                    q, k_ref[:, mine], dims, preferred_element_type=jnp.float32) * scale, -jnp.inf)
+            ]
+            for s in range(SLOTS):
+                score = lax.dot_general(
+                    q, slots[s, :, kcols], dims, preferred_element_type=jnp.float32) * scale
+                scores.append(jnp.where(masks[s], score, -jnp.inf))
+            top = functools.reduce(jnp.maximum, scores)
+            top = jnp.max(top, axis=1, keepdims=True)
+            weights = [jnp.exp(s - top) for s in scores]
+            total = jnp.sum(functools.reduce(jnp.add, weights), axis=1, keepdims=True)
+            mixed = jnp.dot(weights[0].astype(jnp.bfloat16), v_ref[:, mine],
+                            preferred_element_type=jnp.float32)
+            for s in range(SLOTS):
+                mixed = mixed + jnp.dot(weights[s + 1].astype(jnp.bfloat16), slots[s, :, vcols],
+                                        preferred_element_type=jnp.float32)
+            mixed = jnp.where(keep_row, mixed / total, 0.0)
+            att_ref[:, mine] = mixed.astype(jnp.bfloat16)
+
+    for ch in range(CHUNKS):
+        relay(ch)
+        if ch == CHUNKS - 1:
+            origin = lax.rem(me + 12, 16)
+            rows_of = slots.at[zslot]
+            go((z >= 1) & (x == 0), remote(block(rows_of, lax.rem(my_chip + 1, 8)), got_ref.at[origin],
+                                           send_f.at[0], recv_r.at[origin], lax.rem(me + 2, 16)))
+            for zp in (3, 2):
+                for xp in range(2):
+                    go((z >= 1) & (zp > z), remote(
+                        block(rows_of, 2 * zp + xp), got_ref.at[origin],
+                        send_f.at[1 + 2 * (zp - 2) + xp], recv_r.at[origin],
+                        lax.rem(4 * zp + 2 * xp + c, 16)))
+        if ch >= 1:
+            attention(ch - 1)
+    attention(CHUNKS - 1)
+
+    taken = []
+    for s in range(4):
+        copy = pltpu.make_async_copy(
+            block(slots.at[s], my_chip), got_ref.at[jnp.maximum(spans[s], 0)], local_sem.at[s])
+        pl.when(spans[s] >= 0)(copy.start)
+        taken.append((spans[s] >= 0, copy))
+
+    def landed(source):
+        ref = got_ref.at[source]
+        pltpu.make_async_copy(ref, ref, recv_r.at[source]).wait()
+
+    direct = []
+    for zs in (3, 2, 1, 0):
+        for xs in range(2):
+            cond = (zs > z) | (zs < z - 1)
+            if xs == 1:
+                cond = cond | ((zs == z) & (x == 0))
+            else:
+                cond = cond | ((zs == z - 1) & (x == 1))
+            direct.append((zs, xs, cond))
+    for zs, xs, cond in direct:
+        source = 4 * zs + 2 * xs + c
+
+        @pl.when(cond)
+        def _(source=source):
+            landed(source)
+        go(cond, remote(got_ref.at[source], got_ref.at[source], send_x.at[2 * zs + xs],
+                        recv_r.at[source], sibling))
+    landed(sibling)
+    for zs, xs, cond in direct:
+        source = 4 * zs + 2 * xs + 1 - c
+
+        @pl.when(cond)
+        def _(source=source):
+            landed(source)
+
+    keep.wait()
+    for cond, copy in taken:
+        pl.when(cond)(copy.wait)
+    for cond, copy in started:
+        pl.when(cond)(copy.wait_send)
+
+
+def unpack_kernel(got_ref, att_in, att_out, key_out, value_out):
+    core = lax.axis_index("prefill") % 2
+    cw = key_out.shape[1]
+    r = lax.broadcasted_iota(jnp.int32, (128, 256), 0)
+    t = lax.broadcasted_iota(jnp.int32, (128, 256), 1)
+    moves = jnp.where(t == ((r & 15) << 4) + core * 8 + (r >> 4), 1.0, 0.0).astype(jnp.bfloat16)
+    for out, base in ((key_out, 0), (value_out, cw)):
+        for n in range(cw // 512):
+            out[:, n * 512:(n + 1) * 512] = jnp.dot(
+                moves, got_ref[:, base + n * 512:base + (n + 1) * 512],
+                preferred_element_type=jnp.float32,
+            ).astype(jnp.bfloat16)
+    att_out[...] = att_in[...]
+
+
+def planned(queries, keys, values, span_prompt, tails, owners):
+    rows, width = queries.shape
+    vmem = pl.BlockSpec(memory_space=pltpu.VMEM)
+    smem = pl.BlockSpec(memory_space=pltpu.SMEM)
+    dma = pltpu.SemaphoreType.DMA
+    attended, got = pl.pallas_call(
+        exchange_kernel,
+        out_shape=(
+            jax.ShapeDtypeStruct((rows, width), jnp.bfloat16),
+            jax.ShapeDtypeStruct((16, 16, 2 * width), jnp.bfloat16),
+        ),
+        in_specs=[smem] * 3 + [vmem] * 3,
+        out_specs=(vmem, pl.BlockSpec(memory_space=pl.ANY)),
+        scratch_shapes=[
+            pltpu.VMEM((rows, 2 * width), jnp.bfloat16),
+            pltpu.VMEM((SLOTS, rows, 2 * width), jnp.bfloat16),
+            dma((SLOTS, CHUNKS)),
+            dma((3, CHUNKS)),
+            dma((5, CHUNKS)),
+            dma((16,)),
+            dma((8,)),
+            dma((5,)),
+            dma((8,)),
+            dma((5,)),
+        ],
+        compiler_params=pltpu.CompilerParams(
+            collective_id=0, has_side_effects=True, vmem_limit_bytes=52 * 2**20
+        ),
+        cost_estimate=pl.CostEstimate(
+            flops=24 * rows * rows * width, bytes_accessed=32 * rows * width,
+            transcendentals=MAXC * HEADS * rows * rows,
+        ),
+    )(span_prompt, tails, owners, queries, keys, values)
+    cw = width // CHUNKS
+    return pl.pallas_call(
+        unpack_kernel,
+        grid=(CHUNKS,),
+        out_shape=(jax.ShapeDtypeStruct((rows, width), jnp.bfloat16),) * 3,
+        in_specs=[
+            pl.BlockSpec((256, 2 * cw), lambda n: (0, n)),
+            pl.BlockSpec((rows, cw), lambda n: (0, n)),
+        ],
+        out_specs=(pl.BlockSpec((rows, cw), lambda n: (0, n)),) * 3,
+        compiler_params=pltpu.CompilerParams(vmem_limit_bytes=32 * 2**20),
+    )(got.reshape(256, 2 * width), attended)
+
+
 def solution(mesh):
     placed = (
         P(("groups", "prefill"), None),
@@ -99,7 +401,7 @@
         P("groups"),
     )
     return jax.shard_map(
-        local,
+        planned if mesh.shape["prefill"] == 16 else local,
         mesh=mesh,
         in_specs=placed,
         out_specs=(

time: 364 us -> 211 us (0.58)
  the two profiles are of different devices: /device:TPU:15 before, /device:TPU:19 now
where the time goes in v1:
time: 211 us
  Pallas kernels  203 us (96%)
  local copies, waits for them, and re-layouts  6.92 us (3%)
    pallas_call x1, Pallas kernels, planned(): pl.pallas_call(exchange_kernel, out_shape=(jax.ShapeDtypeStruct((rows, wi...  199 us
    unnamed x10, local copies, waits for them, and re-layouts  6.92 us

profile of v1, /device:TPU:19, one launch (start us, length us, event | category | flops | bytes accessed | tf_op | source)
XLA Modules:
  0.0 210.6 jit_solution(8596281474158114458)
XLA Ops:
  0.6 0.0 copy-start.2
  0.6 0.6 copy-done.2
  1.3 0.0 copy-start.3
  1.3 0.7 copy-done.3
  1.9 0.0 copy-start.4
  1.9 0.7 copy-done.4
  2.6 199.1 %shard_map.85 = (bf16[128,8192]{1,0:T(8,128)(2,1)}, bf16[16,16,16384]{2,1,0:T(8,128)(2,1)}) custom-call(s32[16]{0:T(128)S(1)} %copy-done.2, s32[5]{0:T(128)S(1)} %copy-done.3, s32[5]{0:T(128)S(1)} %copy-done.4, bf16[128,8192]{1,0:T(8,128)(2,1)} %q_ref.1, bf16[128,8192]{1,0:T(8,128)(2,1)} %k_ref.1, bf16[128,8192]{1,0:T(8,128)(2,1)} %v_ref.1), custom_call_target="tpu_custom_call" | custom-call | flops 3221225472 | bytes 33554432 | tf_op jit(solution)/shard_map/pallas_call | solution.py:352
  201.7 0.0 copy-start
  201.7 3.4 %copy-done = bf16[16,16,16384]{2,1,0:T(8,128)(2,1)S(1)} copy-done((bf16[16,16,16384]{2,1,0:T(8,128)(2,1)S(1)}, bf16[16,16,16384]{2,1,0:T(8,128)(2,1)}, u32[]{:S(2)}) %copy-start) | copy-done | bytes 8388632
  205.1 0.0 copy-start.1
  205.1 1.6 copy-done.1
  206.7 3.9 %shard_map.86 = (bf16[128,8192]{1,0:T(8,128)(2,1)}, bf16[128,8192]{1,0:T(8,128)(2,1)}, bf16[128,8192]{1,0:T(8,128)(2,1)}) custom-call(bf16[256,16384]{1,0:T(8,128)(2,1)S(1)} %bitcast.1, bf16[128,8192]{1,0:T(8,128)(2,1)S(1)} %copy-done.1), custom_call_target="tpu_custom_call" | custom-call | tf_op jit(solution)/shard_map/pallas_call | solution.py:381
Async XLA Ops:
  0.6 0.7 copy-start.2
  1.3 0.7 copy-start.3
  1.9 0.7 copy-start.4
  201.7 3.4 %copy-start = (bf16[16,16,16384]{2,1,0:T(8,128)(2,1)S(1)}, bf16[16,16,16384]{2,1,0:T(8,128)(2,1)}, u32[]{:S(2)}) copy-start(bf16[16,16,16384]{2,1,0:T(8,128)(2,1)} %get-tuple-element.5) | copy-start | bytes 25165828
  205.1 1.6 copy-start.1

commit v2 on v1

--- a/solution.py
+++ b/solution.py
@@ -97,7 +97,7 @@
 
 def exchange_kernel(
     sp, tails, owners, q_ref, k_ref, v_ref, att_ref, got_ref,
-    packed, slots, recv, send_a, send_b, recv_r, send_r, send_f, send_x, local_sem,
+    packed, slots, recv, send_a, send_b, recv_r, send_r, send_f, send_g, send_x, local_sem,
 ):
     rows, width = q_ref.shape
     depth = width // HEADS
@@ -217,9 +217,14 @@
         def _():
             arrived(second, ch)
         there = slots.at[second, :, cols(ch)]
-        go((x == 0) & (z >= 1) & (z < 3) & (c == 1),
-           remote(there, slots.at[4, :, cols(ch)], send_b.at[3, ch], recv.at[4, ch],
-                  lax.rem(me + 3, 16)))
+        if ch < CHUNKS - 1:
+            go((x == 0) & (z >= 1) & (z < 3) & (c == 1),
+               remote(there, slots.at[4, :, cols(ch)], send_b.at[3, ch], recv.at[4, ch],
+                      lax.rem(me + 3, 16)))
+        else:
+            go((x == 1) & (z >= 1) & (z < 3) & (c == 1),
+               remote(here, slots.at[4, :, cols(ch)], send_b.at[3, ch], recv.at[4, ch],
+                      lax.rem(me + 1, 16)))
         go(has, remote(there, slots.at[second, :, cols(ch)], send_b.at[4, ch],
                        recv.at[second, ch], sibling))
 
@@ -237,9 +242,10 @@
         def _():
             arrived(2 * (1 - x) + (1 - c), ch)
 
-        @pl.when(spans[4] >= 0)
-        def _():
-            arrived(4, ch)
+        if ch < CHUNKS - 1:
+            @pl.when(spans[4] >= 0)
+            def _():
+                arrived(4, ch)
 
         @pl.loop(0, HEADS // CHUNKS)
         def _(n):
@@ -274,16 +280,37 @@
         if ch == CHUNKS - 1:
             origin = lax.rem(me + 12, 16)
             rows_of = slots.at[zslot]
-            go((z >= 1) & (x == 0), remote(block(rows_of, lax.rem(my_chip + 1, 8)), got_ref.at[origin],
-                                           send_f.at[0], recv_r.at[origin], lax.rem(me + 2, 16)))
+            go((z >= 1) & (x == 0) & (c == 0), remote(
+                block(rows_of, lax.rem(my_chip + 1, 8)), got_ref.at[origin],
+                send_f.at[0], recv_r.at[origin], lax.rem(me + 2, 16)))
             for zp in (3, 2):
                 for xp in range(2):
-                    go((z >= 1) & (zp > z), remote(
+                    go((z >= 1) & (zp > z) & (c == 0), remote(
                         block(rows_of, 2 * zp + xp), got_ref.at[origin],
                         send_f.at[1 + 2 * (zp - 2) + xp], recv_r.at[origin],
-                        lax.rem(4 * zp + 2 * xp + c, 16)))
+                        4 * zp + 2 * xp + c))
         if ch >= 1:
             attention(ch - 1)
+
+    @pl.when(spans[4] >= 0)
+    def _():
+        arrived(4, CHUNKS - 1)
+    fifth = jnp.maximum(spans[4], 0)
+    has_fifth = (c == 0) & (spans[4] >= 0)
+    for zp in (3, 2):
+        for xp in range(2):
+            go(has_fifth & (zp > z), remote(
+                block(slots.at[4], 2 * zp + xp), got_ref.at[fifth],
+                send_g.at[2 * (zp - 2) + xp], recv_r.at[fifth],
+                4 * zp + 2 * xp + 1 - c))
+    go(has_fifth & (x == 0), remote(
+        block(slots.at[4], lax.rem(my_chip + 1, 8)), got_ref.at[fifth],
+        send_g.at[4], recv_r.at[fifth], lax.rem(me + 3, 16)))
+    go(has_fifth, remote(block(slots.at[4], my_chip), got_ref.at[fifth], send_g.at[5],
+                         recv_r.at[fifth], sibling))
+    own_fifth = pltpu.make_async_copy(block(slots.at[4], my_chip), got_ref.at[fifth],
+                                      local_sem.at[5])
+    pl.when(has_fifth)(own_fifth.start)
     attention(CHUNKS - 1)
 
     taken = []
@@ -297,31 +324,37 @@
         ref = got_ref.at[source]
         pltpu.make_async_copy(ref, ref, recv_r.at[source]).wait()
 
-    direct = []
-    for zs in (3, 2, 1, 0):
-        for xs in range(2):
-            cond = (zs > z) | (zs < z - 1)
-            if xs == 1:
-                cond = cond | ((zs == z) & (x == 0))
-            else:
-                cond = cond | ((zs == z - 1) & (x == 1))
-            direct.append((zs, xs, cond))
-    for zs, xs, cond in direct:
+    def direct(zs, xs, core):
+        cond = zs > z
+        if xs == 1:
+            cond = cond | ((zs == z) & (x == 0))
+            cond = cond | (zs < z - 2) | ((zs == z - 2) & ((x == 1) | (core == 0)))
+        else:
+            cond = cond | ((zs == z - 1) & (x == 1) & (core == 0)) | (zs < z - 1)
+        return cond
+
+    chips = [(zs, xs) for zs in (3, 2, 1, 0) for xs in range(2)]
+    for zs, xs in chips:
         source = 4 * zs + 2 * xs + c
 
-        @pl.when(cond)
+        @pl.when(direct(zs, xs, c))
         def _(source=source):
             landed(source)
-        go(cond, remote(got_ref.at[source], got_ref.at[source], send_x.at[2 * zs + xs],
-                        recv_r.at[source], sibling))
+        go(direct(zs, xs, c), remote(got_ref.at[source], got_ref.at[source],
+                                     send_x.at[2 * zs + xs], recv_r.at[source], sibling))
     landed(sibling)
-    for zs, xs, cond in direct:
+
+    @pl.when((c == 1) & (me >= 6))
+    def _():
+        landed(jnp.maximum(me - 6, 0))
+    for zs, xs in chips:
         source = 4 * zs + 2 * xs + 1 - c
 
-        @pl.when(cond)
+        @pl.when(direct(zs, xs, 1 - c))
         def _(source=source):
             landed(source)
 
+    pl.when(has_fifth)(own_fifth.wait)
     keep.wait()
     for cond, copy in taken:
         pl.when(cond)(copy.wait)
@@ -366,8 +399,9 @@
             dma((16,)),
             dma((8,)),
             dma((5,)),
+            dma((6,)),
             dma((8,)),
-            dma((5,)),
+            dma((6,)),
         ],
         compiler_params=pltpu.CompilerParams(
             collective_id=0, has_side_effects=True, vmem_limit_bytes=52 * 2**20

time: 211 us -> 219 us (1.038)
  Pallas kernels: 203 us -> 211 us
    pallas_call x1, Pallas kernels: 199 us -> 207 us  [planned(): pl.pallas_call(exchange_kernel, out_shape=(jax.ShapeDtypeStruct((rows, wi...]
where the time goes in v2:
time: 219 us; the launch traced here: 218 us
  Pallas kernels  211 us (96%)
  local copies, waits for them, and re-layouts  6.92 us (3%)
    pallas_call x1, Pallas kernels, planned(): pl.pallas_call(exchange_kernel, out_shape=(jax.ShapeDtypeStruct((rows, wi...  207 us
    unnamed x10, local copies, waits for them, and re-layouts  6.92 us

profile of v2, /device:TPU:19, one launch (start us, length us, event | category | flops | bytes accessed | tf_op | source)
XLA Modules:
  0.0 218.3 jit_solution(18411804374605362255)
XLA Ops:
  0.6 0.0 copy-start.2
  0.6 0.6 copy-done.2
  1.3 0.0 copy-start.3
  1.3 0.7 copy-done.3
  1.9 0.0 copy-start.4
  1.9 0.7 copy-done.4
  2.6 206.8 %shard_map.85 = (bf16[128,8192]{1,0:T(8,128)(2,1)}, bf16[16,16,16384]{2,1,0:T(8,128)(2,1)}) custom-call(s32[16]{0:T(128)S(1)} %copy-done.2, s32[5]{0:T(128)S(1)} %copy-done.3, s32[5]{0:T(128)S(1)} %copy-done.4, bf16[128,8192]{1,0:T(8,128)(2,1)} %q_ref.1, bf16[128,8192]{1,0:T(8,128)(2,1)} %k_ref.1, bf16[128,8192]{1,0:T(8,128)(2,1)} %v_ref.1), custom_call_target="tpu_custom_call" | custom-call | flops 3221225472 | bytes 33554432 | tf_op jit(solution)/shard_map/pallas_call | solution.py:385
  209.5 0.0 copy-start
  209.5 3.4 %copy-done = bf16[16,16,16384]{2,1,0:T(8,128)(2,1)S(1)} copy-done((bf16[16,16,16384]{2,1,0:T(8,128)(2,1)S(1)}, bf16[16,16,16384]{2,1,0:T(8,128)(2,1)}, u32[]{:S(2)}) %copy-start) | copy-done | bytes 8388632
  212.8 0.0 copy-start.1
  212.8 1.6 copy-done.1
  214.4 3.9 %shard_map.86 = (bf16[128,8192]{1,0:T(8,128)(2,1)}, bf16[128,8192]{1,0:T(8,128)(2,1)}, bf16[128,8192]{1,0:T(8,128)(2,1)}) custom-call(bf16[256,16384]{1,0:T(8,128)(2,1)S(1)} %bitcast.1, bf16[128,8192]{1,0:T(8,128)(2,1)S(1)} %copy-done.1), custom_call_target="tpu_custom_call" | custom-call | tf_op jit(solution)/shard_map/pallas_call | solution.py:415
Async XLA Ops:
  0.6 0.7 copy-start.2
  1.3 0.7 copy-start.3
  1.9 0.7 copy-start.4
  209.5 3.4 %copy-start = (bf16[16,16,16384]{2,1,0:T(8,128)(2,1)S(1)}, bf16[16,16,16384]{2,1,0:T(8,128)(2,1)}, u32[]{:S(2)}) copy-start(bf16[16,16,16384]{2,1,0:T(8,128)(2,1)} %get-tuple-element.5) | copy-start | bytes 25165828
  212.8 1.6 copy-start.1

commit v3 on v2

--- a/solution.py
+++ b/solution.py
@@ -1,4 +1,5 @@
 import functools
+import math
 import jax
 import jax.numpy as jnp
 from jax import lax
@@ -8,8 +9,10 @@
 
 HEADS = 64
 MAXC = 6
-CHUNKS = 4
+CHUNKS = 8
 SLOTS = 5
+TOGETHER = 4
+AHEAD = 4
 MESH = pl.DeviceIdType.MESH
 
 
@@ -97,7 +100,7 @@
 
 def exchange_kernel(
     sp, tails, owners, q_ref, k_ref, v_ref, att_ref, got_ref,
-    packed, slots, recv, send_a, send_b, recv_r, send_r, send_f, send_g, send_x, local_sem,
+    packed, slots, recv, send_a, send_b, recv_r, send_r, send_f, send_g, send_h, send_x, local_sem,
 ):
     rows, width = q_ref.shape
     depth = width // HEADS
@@ -184,6 +187,9 @@
     def block(ref, chip):
         return ref.at[pl.ds(pl.multiple_of(chip * 16, 16), 16), :]
 
+    def piece(slot, chip, ch):
+        return slots.at[slot, pl.ds(pl.multiple_of(chip * 16, 16), 16), cols(ch)]
+
     my_chip = me // 2
     keep = pltpu.make_async_copy(block(packed, my_chip), got_ref.at[me], local_sem.at[4])
     keep.start()
@@ -192,8 +198,9 @@
                       recv_r.at[me], lax.rem(me + 14, 16)))
     for zp in (2, 1, 0):
         for xp in range(2):
-            go(zp < z, remote(block(packed, 2 * zp + xp), got_ref.at[me], send_r.at[2 * zp + xp],
-                              recv_r.at[me], lax.rem(4 * zp + 2 * xp + c, 16)))
+            go((zp < z) & ((x == 1) | (xp == 0)), remote(
+                block(packed, 2 * zp + xp), got_ref.at[me], send_r.at[2 * zp + xp],
+                recv_r.at[me], 4 * zp + 2 * xp + c))
 
     def arrived(slot, ch):
         ref = slots.at[slot, :, cols(ch)]
@@ -210,6 +217,20 @@
                                                   recv.at[4, ch], lax.rem(me + 1, 16)))
         go(z >= 1, remote(here, slots.at[zslot, :, cols(ch)], send_b.at[2, ch],
                           recv.at[zslot, ch], sibling))
+        origin = lax.rem(me + 12, 16)
+        into = got_ref.at[origin, :, cols(ch)]
+        go((z >= 1) & (x == 0) & (c == 0), remote(
+            piece(zslot, lax.rem(my_chip + 1, 8), ch), into,
+            send_f.at[0, ch], recv_r.at[origin], lax.rem(me + 2, 16)))
+        for zp in (3, 2):
+            for xp in range(2):
+                cond = (z >= 1) & (zp > z) & (c == 0)
+                if zp == 3 and xp == 1:
+                    cond = cond & ((z < 2) | (x == 1))
+                go(cond, remote(
+                    piece(zslot, 2 * zp + xp, ch), into,
+                    send_f.at[1 + 2 * (zp - 2) + xp, ch], recv_r.at[origin],
+                    4 * zp + 2 * xp + c))
         second = 2 * (1 - x) + c
         has = (x == 1) | (z >= 1)
 
@@ -217,7 +238,7 @@
         def _():
             arrived(second, ch)
         there = slots.at[second, :, cols(ch)]
-        if ch < CHUNKS - 1:
+        if ch < CHUNKS * 3 // 4:
             go((x == 0) & (z >= 1) & (z < 3) & (c == 1),
                remote(there, slots.at[4, :, cols(ch)], send_b.at[3, ch], recv.at[4, ch],
                       lax.rem(me + 3, 16)))
@@ -227,11 +248,22 @@
                       lax.rem(me + 1, 16)))
         go(has, remote(there, slots.at[second, :, cols(ch)], send_b.at[4, ch],
                        recv.at[second, ch], sibling))
-
-    scale = 1.0 / depth**0.5
+        go((z == 1) & (x == 1) & (c == 0), remote(
+            piece(second, 7, ch), got_ref.at[lax.rem(me + 14, 16), :, cols(ch)],
+            send_h.at[3, ch], recv_r.at[lax.rem(me + 14, 16)], 14))
+        origin = lax.rem(me + 14, 16)
+        for zp in (2, 1, 0):
+            go((x == 1) & (zp < z), remote(
+                piece(second, 2 * zp + 1, ch), got_ref.at[origin, :, cols(ch)],
+                send_h.at[zp, ch], recv_r.at[origin], 4 * zp + 2 + c))
+
+    scale = math.log2(math.e) / depth**0.5
     causal = (t <= r) & (t < used_rows)
     keep_row = lax.broadcasted_iota(jnp.int32, (rows, depth), 0) < used_rows
     masks = [jnp.full((rows, rows), f, jnp.int32) > 0 for f in flags]
+
+    fifth = jnp.maximum(spans[4], 0)
+    has_fifth = (c == 0) & (spans[4] >= 0)
 
     def attention(ch):
         @pl.when(z >= 1)
@@ -242,14 +274,23 @@
         def _():
             arrived(2 * (1 - x) + (1 - c), ch)
 
-        if ch < CHUNKS - 1:
-            @pl.when(spans[4] >= 0)
-            def _():
-                arrived(4, ch)
-
-        @pl.loop(0, HEADS // CHUNKS)
-        def _(n):
-            at = pl.multiple_of(n * depth, depth)
+        @pl.when(spans[4] >= 0)
+        def _():
+            arrived(4, ch)
+        into = got_ref.at[fifth, :, cols(ch)]
+        for zp in (3, 2):
+            for xp in range(2):
+                go(has_fifth & (zp > z), remote(
+                    piece(4, 2 * zp + xp, ch), into,
+                    send_g.at[2 * (zp - 2) + xp, ch], recv_r.at[fifth],
+                    4 * zp + 2 * xp + 1 - c))
+        go(has_fifth & (x == 0), remote(
+            piece(4, lax.rem(my_chip + 1, 8), ch), into,
+            send_g.at[4, ch], recv_r.at[fifth], lax.rem(me + 3, 16)))
+        go(has_fifth, remote(piece(4, my_chip, ch), into, send_g.at[5, ch],
+                             recv_r.at[fifth], sibling))
+
+        def head(at):
             mine = pl.ds(ch * cw + at, depth)
             kcols = pl.ds(2 * ch * cw + at, depth)
             vcols = pl.ds((2 * ch + 1) * cw + at, depth)
@@ -257,15 +298,15 @@
             dims = (((1,), (1,)), ((), ()))
             scores = [
                 jnp.where(causal, lax.dot_general(
-                    q, k_ref[:, mine], dims, preferred_element_type=jnp.float32) * scale, -jnp.inf)
+                    q, k_ref[:, mine], dims, preferred_element_type=jnp.float32), -jnp.inf)
             ]
             for s in range(SLOTS):
                 score = lax.dot_general(
-                    q, slots[s, :, kcols], dims, preferred_element_type=jnp.float32) * scale
+                    q, slots[s, :, kcols], dims, preferred_element_type=jnp.float32)
                 scores.append(jnp.where(masks[s], score, -jnp.inf))
             top = functools.reduce(jnp.maximum, scores)
             top = jnp.max(top, axis=1, keepdims=True)
-            weights = [jnp.exp(s - top) for s in scores]
+            weights = [jnp.exp2((s - top) * scale) for s in scores]
             total = jnp.sum(functools.reduce(jnp.add, weights), axis=1, keepdims=True)
             mixed = jnp.dot(weights[0].astype(jnp.bfloat16), v_ref[:, mine],
                             preferred_element_type=jnp.float32)
@@ -275,44 +316,20 @@
             mixed = jnp.where(keep_row, mixed / total, 0.0)
             att_ref[:, mine] = mixed.astype(jnp.bfloat16)
 
-    for ch in range(CHUNKS):
-        relay(ch)
-        if ch == CHUNKS - 1:
-            origin = lax.rem(me + 12, 16)
-            rows_of = slots.at[zslot]
-            go((z >= 1) & (x == 0) & (c == 0), remote(
-                block(rows_of, lax.rem(my_chip + 1, 8)), got_ref.at[origin],
-                send_f.at[0], recv_r.at[origin], lax.rem(me + 2, 16)))
-            for zp in (3, 2):
-                for xp in range(2):
-                    go((z >= 1) & (zp > z) & (c == 0), remote(
-                        block(rows_of, 2 * zp + xp), got_ref.at[origin],
-                        send_f.at[1 + 2 * (zp - 2) + xp], recv_r.at[origin],
-                        4 * zp + 2 * xp + c))
-        if ch >= 1:
-            attention(ch - 1)
-
-    @pl.when(spans[4] >= 0)
-    def _():
-        arrived(4, CHUNKS - 1)
-    fifth = jnp.maximum(spans[4], 0)
-    has_fifth = (c == 0) & (spans[4] >= 0)
-    for zp in (3, 2):
-        for xp in range(2):
-            go(has_fifth & (zp > z), remote(
-                block(slots.at[4], 2 * zp + xp), got_ref.at[fifth],
-                send_g.at[2 * (zp - 2) + xp], recv_r.at[fifth],
-                4 * zp + 2 * xp + 1 - c))
-    go(has_fifth & (x == 0), remote(
-        block(slots.at[4], lax.rem(my_chip + 1, 8)), got_ref.at[fifth],
-        send_g.at[4], recv_r.at[fifth], lax.rem(me + 3, 16)))
-    go(has_fifth, remote(block(slots.at[4], my_chip), got_ref.at[fifth], send_g.at[5],
-                         recv_r.at[fifth], sibling))
+        @pl.loop(0, HEADS // CHUNKS // TOGETHER)
+        def _(n):
+            for m in range(TOGETHER):
+                head(pl.multiple_of((n * TOGETHER + m) * depth, depth))
+
+    for ch in range(CHUNKS + AHEAD):
+        if ch < CHUNKS:
+            relay(ch)
+        if ch >= AHEAD:
+            attention(ch - AHEAD)
+
     own_fifth = pltpu.make_async_copy(block(slots.at[4], my_chip), got_ref.at[fifth],
                                       local_sem.at[5])
     pl.when(has_fifth)(own_fifth.start)
-    attention(CHUNKS - 1)
-
     taken = []
     for s in range(4):
         copy = pltpu.make_async_copy(
@@ -398,8 +415,9 @@
             dma((5, CHUNKS)),
             dma((16,)),
             dma((8,)),
-            dma((5,)),
-            dma((6,)),
+            dma((5, CHUNKS)),
+            dma((6, CHUNKS)),
+            dma((4, CHUNKS)),
             dma((8,)),
             dma((6,)),
         ],

time: 219 us -> 190 us (0.87)
  the two profiles are of different devices: /device:TPU:19 before, /device:TPU:29 now
where the time goes in v3:
time: 190 us
  Pallas kernels  182 us (96%)
  local copies, waits for them, and re-layouts  6.92 us (4%)
    pallas_call x1, Pallas kernels, planned(): pl.pallas_call(exchange_kernel, out_shape=(jax.ShapeDtypeStruct((rows, wi...  177 us
    unnamed x10, local copies, waits for them, and re-layouts  6.92 us
    pallas_call x1, Pallas kernels, planned(): pl.pallas_call(unpack_kernel, grid=(CHUNKS,), out_shape=(jax.ShapeDtypeSt...  5.22 us

profile of v3, /device:TPU:29, one launch (start us, length us, event | category | flops | bytes accessed | tf_op | source)
XLA Modules:
  0.0 189.9 jit_solution(12799963192422451037)
XLA Ops:
  0.6 0.0 copy-start.2
  0.6 0.6 copy-done.2
  1.3 0.0 copy-start.3
  1.3 0.7 copy-done.3
  1.9 0.0 copy-start.4
  1.9 0.7 copy-done.4
  2.6 177.1 %shard_map.85 = (bf16[128,8192]{1,0:T(8,128)(2,1)}, bf16[16,16,16384]{2,1,0:T(8,128)(2,1)}) custom-call(s32[16]{0:T(128)S(1)} %copy-done.2, s32[5]{0:T(128)S(1)} %copy-done.3, s32[5]{0:T(128)S(1)} %copy-done.4, bf16[128,8192]{1,0:T(8,128)(2,1)} %q_ref.1, bf16[128,8192]{1,0:T(8,128)(2,1)} %k_ref.1, bf16[128,8192]{1,0:T(8,128)(2,1)} %v_ref.1), custom_call_target="tpu_custom_call" | custom-call | flops 3221225472 | bytes 33554432 | tf_op jit(solution)/shard_map/pallas_call | solution.py:402
  179.7 0.0 copy-start
  179.7 3.4 %copy-done = bf16[16,16,16384]{2,1,0:T(8,128)(2,1)S(1)} copy-done((bf16[16,16,16384]{2,1,0:T(8,128)(2,1)S(1)}, bf16[16,16,16384]{2,1,0:T(8,128)(2,1)}, u32[]{:S(2)}) %copy-start) | copy-done | bytes 8388632
  183.1 0.0 copy-start.1
  183.1 1.6 copy-done.1
  184.7 5.2 %shard_map.86 = (bf16[128,8192]{1,0:T(8,128)(2,1)}, bf16[128,8192]{1,0:T(8,128)(2,1)}, bf16[128,8192]{1,0:T(8,128)(2,1)}) custom-call(bf16[256,16384]{1,0:T(8,128)(2,1)S(1)} %bitcast.1, bf16[128,8192]{1,0:T(8,128)(2,1)S(1)} %copy-done.1), custom_call_target="tpu_custom_call" | custom-call | tf_op jit(solution)/shard_map/pallas_call | solution.py:433
Async XLA Ops:
  0.6 0.7 copy-start.2
  1.3 0.7 copy-start.3
  1.9 0.7 copy-start.4
  179.7 3.4 %copy-start = (bf16[16,16,16384]{2,1,0:T(8,128)(2,1)S(1)}, bf16[16,16,16384]{2,1,0:T(8,128)(2,1)}, u32[]{:S(2)}) copy-start(bf16[16,16,16384]{2,1,0:T(8,128)(2,1)} %get-tuple-element.5) | copy-start | bytes 25165828
  183.1 1.6 copy-start.1
